TPU v7x, 128 devices: a whole 4x4x4 slice. The times are simulated.
128 devices in a mesh: dp: 2 (over core), segment: 2 (over x_hi), tensor: 32 (over y, x_lo, z).
Axes of the slice: x: 4 (x_hi: 2, x_lo: 2; x = x_hi * 2 + x_lo), y: 4, z: 4, core: 2. Of those that a mesh axis runs over, the one named last changes fastest.
Arguments:
- hidden_state: bfloat16 [256, 16384], P('dp', 'tensor'), parts along dimension 0, may hold values from -6 to 6
- norm_gain: bfloat16 [2, 16384], P('segment'), may hold values from 0.099609375 to 1.8984375
- w_query: bfloat16 [2, 16384, 8192], P('segment', None, 'tensor'), may hold values from -0.046875 to 0.046875
- w_key_value: bfloat16 [2, 16384, 1024], P('segment', 'tensor'), may hold values from -0.046875 to 0.046875
- w_output: bfloat16 [2, 8192, 16384], P('segment', 'tensor'), may hold values from -0.5 to 0.5
- kv_cache: bfloat16 [2, 256, 2, 4, 2048, 128], P('segment', ('dp', 'tensor')), parts along dimension 1, may hold values from -250 to 250
- context_len: int32 [256], P('dp'), parts along dimension 0, may hold values from 2 to 2048, as said below
Outputs:
- section_out: bfloat16 [2, 256, 16384], P('segment', 'dp', 'tensor'), parts along dimension 1
There are 2 independent parts, one for each index of `dp`. A program takes and returns all parts, laid end to end along the dimension named above; an argument that names none is the same for every part. Nothing has to cross between parts.
Inputs may be any that keep to these rules, and one draw needn't show every extreme that they name: `context_len`: each row's context length; at least one row has the full 4 * 512.
All inputs are finite; a program needn't handle non-finite values.
Results may differ from a plain program's by a relative error of at most 0.015.
The roundings to bfloat16 on the way count: a program that leaves them out, or rounds other values in their place, can miss the bound.
Values may be sent and summed in bfloat16 or wider, within the bound.
A program may use at most 192 MiB of HBM per device.

v0:
```python
import jax
import jax.numpy as jnp
from jax import lax
from jax.sharding import PartitionSpec as P

HEADS = 64
KVH = 4
HD = 128


epsilon = 1e-05
masked_value = -1e30


def from_behind(block, axis, distance):
    devices = range(lax.axis_size(axis))
    route = [(i - distance, i) for i in devices if i - distance in devices]
    return lax.ppermute(block, axis, route)


def normalize(inputs, gain):
    values = inputs.astype(jnp.float32)
    mean_square = jnp.mean(values * values, axis=-1, keepdims=True)
    return (values * lax.rsqrt(mean_square + epsilon) * gain.astype(jnp.float32)).astype(
        jnp.bfloat16
    )


def attend(queries, new_entries, keys, values, context_len):
    rows = queries.shape[0]
    grouped = queries.reshape(rows, KVH, HEADS // KVH, HD)
    new_keys = new_entries[:, : KVH * HD].reshape(rows, KVH, HD)
    new_values = new_entries[:, KVH * HD :].reshape(rows, KVH, HD).astype(jnp.float32)
    scale = HD ** (-0.5)
    scores = (
        jnp.einsum("rkgd,rktd->rkgt", grouped, keys, preferred_element_type=jnp.float32) * scale
    )
    own_score = (
        jnp.einsum("rkgd,rkd->rkg", grouped, new_keys, preferred_element_type=jnp.float32) * scale
    )
    position = jnp.arange(keys.shape[2], dtype=jnp.int32)
    visible = (position[None, :] < context_len[:, None])[:, None, None, :]
    scores = jnp.where(visible, scores, masked_value)
    highest = jnp.maximum(jnp.max(scores, axis=-1), own_score)
    raw_weights = jnp.where(visible, jnp.exp(scores - highest[..., None]), 0.0)
    own_raw = jnp.exp(own_score - highest)
    total = jnp.sum(raw_weights, axis=-1) + own_raw
    attention_weights = (raw_weights / total[..., None]).astype(jnp.bfloat16)
    own_weight = (own_raw / total).astype(jnp.bfloat16)
    mixed = jnp.einsum(
        "rkgt,rktd->rkgd", attention_weights, values, preferred_element_type=jnp.float32
    )
    mixed = mixed + own_weight.astype(jnp.float32)[..., None] * new_values[:, :, None, :]
    return mixed.astype(jnp.bfloat16).reshape(rows, HEADS * HD)


def body(hidden_state, norm_gain, w_query, w_key_value, w_output, kv_cache, context_len):
    tensor_index = lax.axis_index("tensor")
    segment_index = lax.axis_index("segment")
    row_share = kv_cache.shape[1]
    width_share = hidden_state.shape[1]
    local_len = lax.dynamic_slice_in_dim(context_len, tensor_index * row_share, row_share)
    gain = norm_gain[0]
    query_weight = w_query[0]
    entry_weight = w_key_value[0]
    output_weight = w_output[0]
    cache = kv_cache[0]

    def section(inputs):
        normed = normalize(inputs, gain)
        queries = jnp.dot(normed, query_weight, preferred_element_type=jnp.float32).astype(
            jnp.bfloat16
        )
        normed_cols = lax.dynamic_slice_in_dim(normed, tensor_index * width_share, width_share, 1)
        new_entries = lax.psum_scatter(
            jnp.dot(normed_cols, entry_weight, preferred_element_type=jnp.float32),
            "tensor",
            scatter_dimension=0,
            tiled=True,
        ).astype(jnp.bfloat16)
        row_queries = lax.all_to_all(queries, "tensor", split_axis=0, concat_axis=1, tiled=True)
        mixed = attend(row_queries, new_entries, cache[:, 0], cache[:, 1], local_len)
        head_mixed = lax.all_to_all(mixed, "tensor", split_axis=1, concat_axis=0, tiled=True)
        return jnp.dot(head_mixed, output_weight, preferred_element_type=jnp.float32)

    whole_input = lax.all_gather(hidden_state, "tensor", axis=1, tiled=True)

    def combine(partial_value):
        return lax.psum(partial_value, "tensor")

    first_whole = (whole_input.astype(jnp.float32) + combine(section(whole_input))).astype(
        jnp.bfloat16
    )
    arrived = from_behind(first_whole, "segment", 1)
    second_whole = (arrived.astype(jnp.float32) + combine(section(arrived))).astype(jnp.bfloat16)
    first_slice = lax.dynamic_slice_in_dim(first_whole, tensor_index * width_share, width_share, 1)
    second_slice = lax.dynamic_slice_in_dim(
        second_whole, tensor_index * width_share, width_share, 1
    )
    result = jnp.where(segment_index == 0, first_slice, second_slice)
    return result[None]


def solution(mesh):
    placed = (
        P("dp", "tensor"),
        P("segment", None),
        P("segment", None, "tensor"),
        P("segment", "tensor", None),
        P("segment", "tensor", None),
        P("segment", ("dp", "tensor"), None, None, None, None),
        P("dp"),
    )
    return jax.shard_map(
        body, mesh=mesh, in_specs=placed, out_specs=P("segment", "dp", "tensor"), check_vma=False
    )
```

profile of v0, /device:TPU:4, one launch (start us, length us, event | category | flops | bytes accessed | tf_op | source)
XLA Modules:
  0.0 1367.8 jit_solution(13668178353248718893)
XLA Ops:
  6.5 0.0 copy-start
  6.5 0.0 all-gather.2.cloned.1.call-start
  6.5 0.7 all-gather.2.cloned.1.call-update
  7.3 0.9 mul.111
  8.2 0.0 copy-start.6
  8.2 0.0 copy-start.5
  8.2 13.7 %copy.26 = bf16[1,4,2,4,2048,128]{5,4,3,1,2,0:T(8,128)(2,1)} copy(bf16[1,4,2,4,2048,128]{5,4,3,2,1,0:T(8,128)(2,1)} %param.12) | data formatting | bytes 33554432 | tf_op args[5]
  22.0 0.0 copy-done.6
  22.0 0.6 dynamic-slice
  23.2 0.0 copy-done.5
  23.2 0.1 dynamic_slice.15
  23.3 0.1 iota_compare_fusion
  23.4 145.4 %all-gather.2.cloned.1.call-done = bf16[128,16384]{1,0:T(8,128)(2,1)} async-done(((bf16[128,512]{1,0:T(8,128)(2,1)}), bf16[128,16384]{1,0:T(8,128)(2,1)}) %all-gather.2.cloned.1.call-update) | async-done | bytes 4194320 | tf_op jit(solution)/shard_map/all_gather | solution.py:86
  168.8 0.0 copy-start.3
  168.8 3.2 fusion
  172.0 0.2 copy-done.3
  172.2 0.0 copy-start.1
  172.2 1.1 fusion.2
  173.3 2.3 copy-done.1
  175.6 1.2 fusion.26
  176.8 0.0 copy-done
  176.9 0.3 fusion.34
  177.2 161.6 %all-reduce.10 = bf16[128,1024]{1,0:T(8,128)(2,1)S(1)} all-reduce(f32[128,1024]{1,0:T(8,128)S(1)} %fusion.34), channel_id=2, replica_groups=mesh['dp'=2,'segment'=2,'tensor'=32] {'tensor'}, use_global_device_ids=true, to_apply=%region_2.3.clone | all-reduce | flops 131072 | bytes 786432
  338.8 0.7 all_to_all.52
  339.4 3.9 all-to-all-start
  343.3 0.0 all-reduce.7.cloned.1.call-start
  343.4 8.4 all-to-all-done
  351.8 0.1 fusion.59
  352.0 5.8 fusion.57
  357.7 0.5 fusion.20
  358.3 4.8 fusion.25
  363.2 0.1 copy.18
  363.2 11.9 all_to_all.70
  375.1 7.9 fusion.6
  383.0 0.0 all-reduce.7.cloned.1.call-update
  383.0 340.0 %all-reduce.7.cloned.1.call-done = f32[128,16384]{1,0:T(8,128)} async-done(((f32[128,16384]{1,0:T(8,128)}), f32[128,16384]{1,0:T(8,128)}) %all-reduce.7.cloned.1.call-update) | async-done | bytes 8388624 | tf_op jit(solution)/shard_map/psum | solution.py:89
  723.0 5.4 fusion.3
  728.4 0.0 copy-start.4
  728.4 1.5 collective-permute-start
  729.9 77.1 %collective-permute-done = bf16[128,16384]{1,0:T(8,128)(2,1)S(1)} collective-permute-done((bf16[128,16384]{1,0:T(8,128)(2,1)S(1)}, bf16[128,16384]{1,0:T(8,128)(2,1)S(1)}, u32[]{:S(2)}, u32[]{:S(2)}) %collective-permute-start) | collective-permute-done | bytes 4194336 | tf_op jit(solution)/shard_map/ppermute | solution.py:18
  806.9 0.0 copy-start.2
  806.9 0.9 multiply_reduce_fusion
  807.8 1.1 multiply_convert_fusion
  808.9 0.0 copy-done.4
  809.0 0.0 copy-done.2
  809.0 4.7 fusion.29
  813.7 0.3 fusion.32
  814.0 160.4 %all-reduce.11 = bf16[128,1024]{1,0:T(8,128)(2,1)S(1)} all-reduce(f32[128,1024]{1,0:T(8,128)S(1)} %fusion.32), channel_id=3, replica_groups=mesh['dp'=2,'segment'=2,'tensor'=32] {'tensor'}, use_global_device_ids=true, to_apply=%region_7.8.clone | all-reduce | flops 131072 | bytes 786432
  974.5 0.7 all_to_all.59
  975.1 3.9 all-to-all-start.2
  979.0 0.0 all-reduce.9.cloned.1.call-start
  979.1 8.4 all-to-all-done.2
  987.5 5.7 fusion.58
  993.3 0.2 fusion.60
  993.4 0.5 fusion.21
  994.0 4.8 fusion.24
  998.9 0.1 copy.20
  998.9 11.9 all_to_all.71
  1010.8 7.9 fusion.4
  1018.7 0.0 all-reduce.9.cloned.1.call-update
  1018.7 6.2 convert_element_type.90
  1025.0 334.5 %all-reduce.9.cloned.1.call-done = f32[128,16384]{1,0:T(8,128)} async-done(((f32[128,16384]{1,0:T(8,128)}), f32[128,16384]{1,0:T(8,128)}) %all-reduce.9.cloned.1.call-update) | async-done | bytes 8388624 | tf_op jit(solution)/shard_map/psum | solution.py:89
  1359.5 1.8 fusion.46
  (22 shorter events, 0.4 us)
Async XLA Ops:
  6.5 170.3 %copy-start = (bf16[1,512,1024]{2,1,0:T(8,128)(2,1)S(1)}, bf16[1,512,1024]{2,1,0:T(8,128)(2,1)}, u32[]{:S(2)}) copy-start(bf16[1,512,1024]{2,1,0:T(8,128)(2,1)} %param.10) | copy-start | bytes 3145732
  6.5 162.2 %all-gather.2.cloned.1.call-start = ((), (), s32[]{:S(2)}) async-start(), calls=%async_computation.4 | async-start | bytes 4325376 | tf_op jit(solution)/shard_map/all_gather | solution.py:86
  8.2 13.8 %copy-start.6 = (u32[128]{0:T(128)S(1)}, u32[128]{0:T(128)}, u32[]{:S(2)}) copy-start(u32[128]{0:T(128)} %constant.41) | copy-start | bytes 1540
  8.2 15.0 %copy-start.5 = (s32[128]{0:T(128)S(1)}, s32[128]{0:T(128)}, u32[]{:S(2)}) copy-start(s32[128]{0:T(128)} %param.13) | copy-start | bytes 1540
  168.8 3.4 copy-start.3
  172.2 3.4 copy-start.1
  339.4 12.3 all-to-all-start
  343.3 379.7 %all-reduce.7.cloned.1.call-start = ((), (), s32[]{:S(2)}) async-start(), calls=%async_computation.5 | async-start | bytes 16777216 | tf_op jit(solution)/shard_map/psum | solution.py:89
  728.4 80.6 %copy-start.4 = (bf16[128,16384]{1,0:T(8,128)(2,1)}, bf16[128,16384]{1,0:T(8,128)(2,1)S(1)}, u32[]{:S(2)}) copy-start(bf16[128,16384]{1,0:T(8,128)(2,1)S(1)} %fusion.3) | copy-start | bytes 12582916
  728.4 78.5 %collective-permute-start = (bf16[128,16384]{1,0:T(8,128)(2,1)S(1)}, bf16[128,16384]{1,0:T(8,128)(2,1)S(1)}, u32[]{:S(2)}, u32[]{:S(2)}) collective-permute-start(bf16[128,16384]{1,0:T(8,128)(2,1)S(1)} %fusion.3), channel_id=1, source_target_pairs={{0,32},{1,33},{2,34},{3,35},{4,36},{5,37},{6,38},{7,39},{8,40},{9,... | collective-permute-start | bytes 12582920 | tf_op jit(solution)/shard_map/ppermute | solution.py:18
  806.9 2.0 copy-start.2
  975.1 12.3 all-to-all-start.2
  979.0 380.5 %all-reduce.9.cloned.1.call-start = ((), (), s32[]{:S(2)}) async-start(), calls=%async_computation.6 | async-start | bytes 16777216 | tf_op jit(solution)/shard_map/psum | solution.py:89
Sparse Core Ops, SparseCore 0:
  9.0 159.7 all-gather.1
  383.1 339.8 all-reduce.6
  1018.8 340.6 all-reduce.8
where the time goes:
time: 1370 us
  waiting for transfers between devices  914 us (67%)
  blocking collectives  346 us (25%)
  matrix products  43.8 us (3%)
  other arithmetic  21.9 us (2%)
  local copies, waits for them, and re-layouts  18.6 us (1%)
  between operations  14.1 us (1%)
    psum x2, waiting for transfers between devices, combine(): return lax.psum(partial_value, 'tensor')  675 us
    unnamed x2, blocking collectives  322 us
    all_gather x1, waiting for transfers between devices, body(): whole_input = lax.all_gather(hidden_state, 'tensor', axis=1, tiled=True)  145 us
    ppermute x1, waiting for transfers between devices, from_behind(): return lax.ppermute(block, axis, route)  77.1 us
  transfers between devices with their start and end apart: 6, of which 6 were waited for; matrix products, arithmetic and copies ran while one was open for 2% of the time, Pallas kernels for 0%

commit v1 on v0

v1 whole, which is shorter than its diff:
```python
import jax
import jax.numpy as jnp
from jax import lax
from jax.experimental import pallas as pl
from jax.experimental.pallas import tpu as pltpu
from jax.sharding import PartitionSpec as P

MESH = pl.DeviceIdType.MESH
D = 16384
KVH = 4
HD = 128
ROWS = 128
N = 32
SHARD = 512
HALF = 256
CTX = 2048
MINE = 4
EPS = 1e-05
MASKED = -1e30
F32 = jnp.float32
BF16 = jnp.bfloat16


def arrived(ref, sem):
    pltpu.make_async_copy(ref, ref, sem).wait()


def kernel(
    hid, gain, wq_hbm, wkv_hbm, wo_hbm, kv_hbm, ctx, out,
    xg, wq, wkv, wo, kvc, qacc,
    st_send, st_recv, nk_tmp, nk_send, nk_recv, nk, q_send, q_recv, m_send, m_recv, mixed,
    s1a, r1a, s1b, r1b, s2a, r2a, s2b, r2b, s3, r3,
    load_sem, ag_send, ag_recv, rs_send, rs_recv, a2a_send, a2a_recv, relay_send, relay_recv,
):
    me = lax.axis_index("tensor")
    seg = lax.axis_index("segment")
    y, x, z = me // 8, (me // 4) % 2, me % 4

    def tid(yy, xx, zz):
        return yy * 8 + xx * 4 + zz

    def sid(h, aa, bb, xx):
        aa, bb = aa % 4, bb % 4
        return tid(bb, xx, aa) if h == 0 else tid(aa, xx, bb)

    ring = [(z, y), (y, z)]
    partner = tid(y, 1 - x, z)
    xs = jnp.where(seg == 0, x, 1 - x)

    def send(src, dst, send_sem, recv_sem, to):
        pltpu.make_async_remote_copy(
            src_ref=src, dst_ref=dst, send_sem=send_sem, recv_sem=recv_sem,
            device_id={"tensor": to}, device_id_type=MESH,
        ).start()

    loads = [
        pltpu.make_async_copy(wkv_hbm.at[0], wkv, load_sem.at[0]),
        pltpu.make_async_copy(wq_hbm.at[0], wq, load_sem.at[1]),
        pltpu.make_async_copy(kv_hbm.at[0], kvc, load_sem.at[2]),
        pltpu.make_async_copy(wo_hbm.at[0], wo, load_sem.at[3]),
    ]
    for copy in loads:
        copy.start()

    @pl.when(seg == 0)
    def _():
        for h in range(2):
            xg[h, me] = hid[:, h * HALF:(h + 1) * HALF]

    barrier = pltpu.get_barrier_semaphore()

    def greet(d, carry):
        pl.semaphore_signal(barrier, inc=1, device_id={"tensor": (me + d) % N}, device_id_type=MESH)
        return carry

    lax.fori_loop(1, N, greet, 0)
    pl.semaphore_signal(
        barrier, inc=1, device_id={"segment": 1 - seg, "tensor": partner}, device_id_type=MESH
    )
    pl.semaphore_wait(barrier, N)

    def along_b(h, j, s):
        a, b = ring[h]
        for dr in range(2):
            k = 1 + 2 * dr + j
            send(xg.at[h, s], xg.at[h, s], ag_send.at[h], ag_recv.at[h, k],
                 sid(h, a, b + 1 - 2 * dr, x))

    def along_a(h, i, s):
        a, b = ring[h]
        for dr in range(2):
            k = 9 + 8 * dr + i
            send(xg.at[h, s], xg.at[h, s], ag_send.at[h], ag_recv.at[h, k],
                 sid(h, a + 1 - 2 * dr, b, x))

    def part(h, s, dr):
        return xg.at[h, s, pl.ds(64 * dr, 64)]

    def turn(g):
        return (3 * g + 3 * ((g * (g - 1)) // 2)) % 4

    def xj(j):
        return (xs + j) % 2

    for h in range(2):
        a, b = ring[h]
        s = sid(h, a, b, xs)

        @pl.when(seg == 1)
        def _():
            arrived(xg.at[h, s], relay_recv.at[h])

        send(xg.at[h, s], xg.at[h, s], ag_send.at[h], ag_recv.at[h, 0], partner)
        along_b(h, 0, s)
        along_a(h, 0, s)

    own = tid(y, xs, z)
    total = jnp.zeros((ROWS, 1), F32)
    for h in range(2):
        v = xg[h, own].astype(F32)
        total = total + jnp.sum(v * v, axis=1, keepdims=True)
    st_send[...] = jnp.broadcast_to(total, (ROWS, 128)).T[0:8]

    def tell_stats(d, carry):
        send(st_send, st_recv.at[me], a2a_send.at[0], a2a_recv.at[0], (me + d) % N)
        return carry

    lax.fori_loop(1, N, tell_stats, 0)
    st_recv[me] = st_send[...]

    for h in range(2):
        a, b = ring[h]
        s = sid(h, a, b, 1 - xs)
        arrived(xg.at[h, s], ag_recv.at[h, 0])
        along_b(h, 1, s)
        along_a(h, 1, s)

    for j in range(2):
        for h in range(2):
            a, b = ring[h]
            for dr in range(2):
                s = sid(h, a, b - 1 + 2 * dr, xj(j))
                arrived(xg.at[h, s], ag_recv.at[h, 1 + 2 * dr + j])
                send(part(h, s, dr), part(h, s, dr), ag_send.at[h], ag_recv.at[h, 5 + 2 * dr + j],
                     sid(h, a, b + 1 - 2 * dr, x))
                along_a(h, 2 + 2 * dr + j, s)

    arrived(st_recv.at[pl.ds(0, N - 1)], a2a_recv.at[0])
    squares = jnp.sum(st_recv[...], axis=0)
    inv = lax.rsqrt(squares[0:1] * (1.0 / D) + EPS)
    inv = jnp.broadcast_to(inv, (ROWS, 128)).T
    inv = jnp.concatenate([inv, inv], axis=1)

    def normed(h, s):
        g = gain[:, pl.ds(pl.multiple_of(s * SHARD + h * HALF, HALF), HALF)].astype(F32)
        return (xg[h, s].astype(F32) * inv * g).astype(BF16)

    loads[0].wait()
    fresh = jnp.concatenate([normed(0, me), normed(1, me)], axis=1)
    for c in range(8):
        piece = jnp.dot(fresh, wkv[:, c * 128:(c + 1) * 128], preferred_element_type=F32)
        nk_tmp[pl.ds(c, ROWS, stride=8), :] = piece
    nk_send[...] = nk_tmp[...].astype(BF16).reshape(N, 32, 128)

    def tell_new(d, carry):
        to = (me + d) % N
        send(nk_send.at[to], nk_recv.at[me], a2a_send.at[1], a2a_recv.at[1], to)
        return carry

    lax.fori_loop(1, N, tell_new, 0)
    nk_recv[me] = nk_send[me]

    for j in range(2):
        for h in range(2):
            a, b = ring[h]
            s = sid(h, a, b + 2, xj(j))
            for dr in range(2):
                arrived(part(h, s, dr), ag_recv.at[h, 5 + 2 * dr + j])
            along_a(h, 6 + j, s)

    loads[1].wait()
    qacc[...] = jnp.zeros_like(qacc)

    def project(h, s):
        w = wq[pl.ds(pl.multiple_of(s * SHARD + h * HALF, HALF), HALF), :]
        return jnp.dot(normed(h, s), w, preferred_element_type=F32)

    def near(i, carry):
        for h in range(2):
            a, b = ring[h]
            bb, xx = b + turn(i // 2), xj(i % 2)
            for dr in range(2):
                s = sid(h, a - 1 + 2 * dr, bb, xx)
                arrived(xg.at[h, s], ag_recv.at[h, 9 + 8 * dr + i])
                send(part(h, s, dr), part(h, s, dr), ag_send.at[h], ag_recv.at[h, 25 + 8 * dr + i],
                     sid(h, a + 1 - 2 * dr, b, x))
            for step in (0, 3, 1):
                qacc[...] += project(h, sid(h, a + step, bb, xx))
        return carry

    lax.fori_loop(0, 8, near, 0)

    def far(i, carry):
        for h in range(2):
            a, b = ring[h]
            s = sid(h, a + 2, b + turn(i // 2), xj(i % 2))
            for dr in range(2):
                arrived(part(h, s, dr), ag_recv.at[h, 25 + 8 * dr + i])
            qacc[...] += project(h, s)
        return carry

    lax.fori_loop(0, 8, far, 0)

    queries = qacc[...].astype(BF16).astype(F32)
    for h in range(2):
        q_send[pl.ds(h, ROWS, stride=2), :] = queries[:, h * HD:(h + 1) * HD]

    def block(ref, t):
        return ref.at[pl.ds(pl.multiple_of(t * 8, 8), 8)]

    def tell_queries(d, carry):
        to = (me + d) % N
        send(block(q_send, to), block(q_recv, me), a2a_send.at[2], a2a_recv.at[2], to)
        return carry

    lax.fori_loop(1, N, tell_queries, 0)
    mine = pl.ds(pl.multiple_of(me * 8, 8), 8)
    q_recv[mine, :] = q_send[mine, :]

    arrived(nk_recv.at[pl.ds(0, N - 1)], a2a_recv.at[1])
    nk[...] = jnp.sum(nk_recv[...].astype(F32), axis=0).astype(BF16).astype(F32)

    loads[2].wait()
    arrived(q_recv.at[pl.ds(0, 8 * (N - 1))], a2a_recv.at[2])

    scale = HD ** (-0.5)

    def attend(r, carry):
        length = ctx[me * MINE + r]
        visible = lax.broadcasted_iota(jnp.int32, (16, CTX), 1) < length
        for k in range(KVH):
            q = jnp.concatenate(
                [q_recv[pl.ds(64 * k + 2 * r + h, 8, stride=8), :] for h in range(2)], axis=0
            )
            new_key = nk[pl.ds(r * 8 + k, 1), :]
            new_value = nk[pl.ds(r * 8 + 4 + k, 1), :]
            scores = lax.dot_general(
                q.astype(BF16), kvc[r, 0, k], (((1,), (1,)), ((), ())), preferred_element_type=F32
            ) * scale
            own_score = jnp.sum(q * new_key, axis=1, keepdims=True) * scale
            scores = jnp.where(visible, scores, MASKED)
            highest = jnp.maximum(jnp.max(scores, axis=1, keepdims=True), own_score)
            raw = jnp.where(visible, jnp.exp(scores - highest), 0.0)
            own_raw = jnp.exp(own_score - highest)
            denom = jnp.sum(raw, axis=1, keepdims=True) + own_raw
            weights = (raw / denom).astype(BF16)
            own_weight = (own_raw / denom).astype(BF16).astype(F32)
            mix = jnp.dot(weights, kvc[r, 1, k], preferred_element_type=F32)
            mix = (mix + own_weight * new_value).astype(BF16).astype(F32)
            for h in range(2):
                m_send[pl.ds(64 * k + 2 * r + h, 8, stride=8), :] = mix[8 * h:8 * h + 8]
        return carry

    lax.fori_loop(0, MINE, attend, 0)

    def tell_mixed(d, carry):
        to = (me + d) % N
        send(block(m_send, to), block(m_recv, me), a2a_send.at[3], a2a_recv.at[3], to)
        return carry

    lax.fori_loop(1, N, tell_mixed, 0)
    m_recv[mine, :] = m_send[mine, :]
    loads[3].wait()
    arrived(m_recv.at[pl.ds(0, 8 * (N - 1))], a2a_recv.at[3])
    for h in range(2):
        mixed[:, h * HD:(h + 1) * HD] = m_recv[pl.ds(h, ROWS, stride=2), :].astype(BF16)

    def partial(h, s):
        w = wo[:, pl.ds(pl.multiple_of(s * SHARD + h * HALF, HALF), HALF)]
        return jnp.dot(mixed[...], w, preferred_element_type=F32)

    def place(b, i):
        return b + turn(3 - i // 2), (x + 1 + i % 2) % 2

    def opposite(i, carry):
        for h in range(2):
            a, b = ring[h]
            bb, xx = place(b, i)
            s1a[h, i] = partial(h, sid(h, a + 2, bb, xx)).astype(BF16)
            for dr in range(2):
                send(s1a.at[h, i, pl.ds(64 * dr, 64)], r1a.at[h, dr, i], rs_send.at[h],
                     rs_recv.at[h, 8 * dr + i], sid(h, a + 1 - 2 * dr, b, x))
        return carry

    lax.fori_loop(0, 8, opposite, 0)

    def merged(value, extra, dr):
        top, low = value[0:64], value[64:128]
        if dr == 0:
            top = top + extra.astype(F32)
        else:
            low = low + extra.astype(F32)
        return jnp.concatenate([top, low], axis=0)

    def beside(i, carry):
        for h in range(2):
            a, b = ring[h]
            bb, xx = place(b, i)
            for dr in range(2):
                value = partial(h, sid(h, a + 1 - 2 * dr, bb, xx))
                arrived(r1a.at[h, dr, i], rs_recv.at[h, 8 * dr + i])
                s1b[h, dr, i] = merged(value, r1a[h, dr, i], dr).astype(BF16)
                send(s1b.at[h, dr, i], r1b.at[h, dr, i], rs_send.at[h],
                     rs_recv.at[h, 16 + 8 * dr + i], sid(h, a + 1 - 2 * dr, b, x))
        return carry

    lax.fori_loop(0, 8, beside, 0)

    def first_ring(h, i):
        a, b = ring[h]
        bb, xx = place(b, i)
        value = partial(h, sid(h, a, bb, xx))
        for dr in range(2):
            arrived(r1b.at[h, dr, i], rs_recv.at[h, 16 + 8 * dr + i])
            value = value + r1b[h, dr, i].astype(F32)
        return value

    def second_opposite(j, carry):
        for h in range(2):
            a, b = ring[h]
            s2a[h, j] = first_ring(h, j).astype(BF16)
            for dr in range(2):
                send(s2a.at[h, j, pl.ds(64 * dr, 64)], r2a.at[h, dr, j], rs_send.at[h],
                     rs_recv.at[h, 32 + 2 * dr + j], sid(h, a, b + 1 - 2 * dr, x))
        return carry

    lax.fori_loop(0, 2, second_opposite, 0)

    def second_beside(j, carry):
        for dr in range(2):
            for h in range(2):
                a, b = ring[h]
                value = first_ring(h, 2 + 2 * dr + j)
                arrived(r2a.at[h, dr, j], rs_recv.at[h, 32 + 2 * dr + j])
                s2b[h, dr, j] = merged(value, r2a[h, dr, j], dr).astype(BF16)
                send(s2b.at[h, dr, j], r2b.at[h, dr, j], rs_send.at[h],
                     rs_recv.at[h, 36 + 2 * dr + j], sid(h, a, b + 1 - 2 * dr, x))
        return carry

    lax.fori_loop(0, 2, second_beside, 0)

    def second_ring(h, j):
        value = first_ring(h, 6 + j)
        for dr in range(2):
            arrived(r2b.at[h, dr, j], rs_recv.at[h, 36 + 2 * dr + j])
            value = value + r2b[h, dr, j].astype(F32)
        return value

    for h in range(2):
        s3[h] = second_ring(h, 0).astype(BF16)
        send(s3.at[h], r3.at[h], rs_send.at[h], rs_recv.at[h, 40], partner)
    for h in range(2):
        value = second_ring(h, 1)
        arrived(r3.at[h], rs_recv.at[h, 40])
        value = value + r3[h].astype(F32) + xg[h, me].astype(F32)
        out[0, :, h * HALF:(h + 1) * HALF] = value.astype(BF16)
        s3[h + 2] = value.astype(BF16)

        @pl.when(seg == 0)
        def _():
            pltpu.make_async_remote_copy(
                src_ref=s3.at[h + 2], dst_ref=xg.at[h, me],
                send_sem=relay_send.at[h], recv_sem=relay_recv.at[h],
                device_id={"segment": 1, "tensor": partner}, device_id_type=MESH,
            ).start()

    for h in range(2):
        blocks = xg.at[h, pl.ds(0, N - 1)]
        arrived(blocks, ag_send.at[h])
        arrived(blocks, rs_send.at[h])

        @pl.when(seg == 0)
        def _():
            arrived(s3.at[h + 2], relay_send.at[h])

    arrived(st_recv.at[pl.ds(0, N - 1)], a2a_send.at[0])
    arrived(nk_recv.at[pl.ds(0, N - 1)], a2a_send.at[1])
    arrived(q_recv.at[pl.ds(0, 8 * (N - 1))], a2a_send.at[2])
    arrived(m_recv.at[pl.ds(0, 8 * (N - 1))], a2a_send.at[3])


def body(hidden_state, norm_gain, w_query, w_key_value, w_output, kv_cache, context_len):
    vmem = pl.BlockSpec(memory_space=pltpu.VMEM)
    hbm = pl.BlockSpec(memory_space=pl.ANY)
    dma = pltpu.SemaphoreType.DMA
    return pl.pallas_call(
        kernel,
        out_shape=jax.ShapeDtypeStruct((1, ROWS, SHARD), BF16),
        in_specs=[vmem, vmem, hbm, hbm, hbm, hbm, pl.BlockSpec(memory_space=pltpu.SMEM)],
        out_specs=vmem,
        scratch_shapes=[
            pltpu.VMEM((2, N, ROWS, HALF), BF16),
            pltpu.VMEM((D, 2 * HD), BF16),
            pltpu.VMEM((SHARD, 2 * KVH * HD), BF16),
            pltpu.VMEM((2 * HD, D), BF16),
            pltpu.VMEM((MINE, 2, KVH, CTX, HD), BF16),
            pltpu.VMEM((ROWS, 2 * HD), F32),
            pltpu.VMEM((8, 128), F32),
            pltpu.VMEM((N, 8, 128), F32),
            pltpu.VMEM((ROWS * 8, 128), F32),
            pltpu.VMEM((N, 32, 128), BF16),
            pltpu.VMEM((N, 32, 128), BF16),
            pltpu.VMEM((32, 128), F32),
            pltpu.VMEM((N * 8, 128), F32),
            pltpu.VMEM((N * 8, 128), F32),
            pltpu.VMEM((N * 8, 128), F32),
            pltpu.VMEM((N * 8, 128), F32),
            pltpu.VMEM((ROWS, 2 * HD), BF16),
            pltpu.VMEM((2, 8, ROWS, HALF), BF16),
            pltpu.VMEM((2, 2, 8, ROWS // 2, HALF), BF16),
            pltpu.VMEM((2, 2, 8, ROWS, HALF), BF16),
            pltpu.VMEM((2, 2, 8, ROWS, HALF), BF16),
            pltpu.VMEM((2, 2, ROWS, HALF), BF16),
            pltpu.VMEM((2, 2, 2, ROWS // 2, HALF), BF16),
            pltpu.VMEM((2, 2, 2, ROWS, HALF), BF16),
            pltpu.VMEM((2, 2, 2, ROWS, HALF), BF16),
            pltpu.VMEM((4, ROWS, HALF), BF16),
            pltpu.VMEM((2, ROWS, HALF), BF16),
            dma((4,)),
            dma((2,)),
            dma((2, 41)),
            dma((2,)),
            dma((2, 41)),
            dma((4,)),
            dma((4,)),
            dma((2,)),
            dma((2,)),
        ],
        compiler_params=pltpu.CompilerParams(
            collective_id=0, has_side_effects=True, vmem_limit_bytes=60 * 1024 * 1024
        ),
    )(hidden_state, norm_gain, w_query, w_key_value, w_output, kv_cache, context_len)


def solution(mesh):
    placed = (
        P("dp", "tensor"),
        P("segment", None),
        P("segment", None, "tensor"),
        P("segment", "tensor", None),
        P("segment", "tensor", None),
        P("segment", ("dp", "tensor"), None, None, None, None),
        P("dp"),
    )
    return jax.shard_map(
        body, mesh=mesh, in_specs=placed, out_specs=P("segment", "dp", "tensor"), check_vma=False
    )
```

time: 1370 us -> 156 us (0.11)
  waiting for transfers between devices: 914 us -> 0 us
  blocking collectives: 346 us -> 0 us
  Pallas kernels: 0 us -> 155 us
  matrix products: 43.8 us -> 0 us
  other arithmetic: 21.9 us -> 0 us
  local copies, waits for them, and re-layouts: 18.6 us -> 1.57 us
  between operations: 14.1 us -> 0.01 us
    psum x2 -> x0, waiting for transfers between devices: 675 us -> none  [combine(): return lax.psum(partial_value, 'tensor')]
    unnamed x2 -> x0, blocking collectives: 322 us -> none
    pallas_call x0 -> x1, Pallas kernels: none -> 155 us  [body(): pl.pallas_call(kernel, out_shape=jax.ShapeDtypeStruct((1, ROWS, SHARD), B...]
    all_gather x1 -> x0, waiting for transfers between devices: 145 us -> none  [body(): whole_input = lax.all_gather(hidden_state, 'tensor', axis=1, tiled=True)]
    ppermute x1 -> x0, waiting for transfers between devices: 77.1 us -> none  [from_behind(): return lax.ppermute(block, axis, route)]
    dot_general x12 -> x0, matrix products: 43.8 us -> none  [the longest x2 15.8 us: section(): jnp.dot(head_mixed, output_weight, preferred_element_type=jnp.float32)]
    all_to_all x2 -> x0, blocking collectives: 23.7 us -> none  [section(): lax.all_to_all(mixed, 'tensor', split_axis=1, concat_axis=0, tiled=True)]
    all_to_all x2 -> x0, waiting for transfers between devices: 16.8 us -> none  [section(): lax.all_to_all(queries, 'tensor', split_axis=0, concat_axis=1, tiled=True)]
  transfers between devices with their start and end apart: 6 -> 0, of which waited for: 6 -> 0; matrix products, arithmetic and copies ran while one was open for 2% -> 0% of each run, Pallas kernels for 0% -> 0%
where the time goes in v1:
time: 156 us
  Pallas kernels  155 us (99%)
  local copies, waits for them, and re-layouts  1.57 us (1%)
    pallas_call x1, Pallas kernels, body(): pl.pallas_call(kernel, out_shape=jax.ShapeDtypeStruct((1, ROWS, SHARD), B...  155 us

profile of v1, /device:TPU:4, one launch (start us, length us, event | category | flops | bytes accessed | tf_op | source)
XLA Modules:
  0.0 156.3 jit_solution(6747430772367705066)
XLA Ops:
  0.0 154.7 %shard_map.73 = bf16[1,128,512]{2,1,0:T(8,128)(2,1)} custom-call(bf16[128,512]{1,0:T(8,128)(2,1)} %hid.1, bf16[1,16384]{1,0:T(2,128)(2,1)} %gain.1, bf16[1,16384,256]{2,1,0:T(8,128)(2,1)} %wq_hbm.1, bf16[1,512,1024]{2,1,0:T(8,128)(2,1)} %wkv_hbm.1, bf16[1,256,16384]{2,1,0:T(8,128)(2,1)} %wo_hbm.1, bf16[1,4,2,4,2048,128]{5,4,3,2,1,0:T(8,128)(2,1)} %kv_hbm.1, ...), custom_call_target="tpu_custom_call" | custom-call | tf_op jit(solution)/shard_map/pallas_call | solution.py:396
  154.7 1.6 %copy.9 = bf16[1,128,512]{2,1,0:T(8,128)(2,1)} copy(bf16[1,128,512]{2,1,0:T(8,128)(2,1)} %shard_map.73) | data formatting | bytes 262144
